TPU v7x, 1024 devices: a whole 4x8x16 slice. The times are simulated.
1024 devices in a mesh: nodes: 64 (over x, z), hidden: 16 (over y, core).
Axes of the slice: x: 4, y: 8, z: 16, core: 2. Of those that a mesh axis runs over, the one named last changes fastest.
Arguments:
- fine_nodes: bfloat16 [131072, 256], P(('nodes', 'hidden')), may hold values from -6 to 6
- fine_edges: bfloat16 [131072, 6, 256], P(('nodes', 'hidden')), may hold values from -6 to 6
- fine_neighbours: int32 [131072, 6], P(('nodes', 'hidden')), may hold values from -1 to 383, as said below
- group_send: int32 [64, 16, 16, 8], P('nodes'), may hold values from 0 to 127
- halo_send: int32 [1024, 64, 2], P(('nodes', 'hidden')), may hold values from 0 to 127
- pool_send: int32 [1024, 64, 4], P(('nodes', 'hidden')), may hold values from -1 to 127, as said below
- pool_recv: int32 [1024, 64, 4], P(('nodes', 'hidden')), may hold values from -1 to 15, as said below
- coarse_neighbours: int32 [16384, 6], P(('nodes', 'hidden')), may hold values from -1 to 15, as said below
- edge_in: bfloat16 [768, 1024], replicated, may hold values from -0.21875 to 0.21875
- edge_out: bfloat16 [1024, 256], replicated, may hold values from -0.1875 to 0.1875
- node_in: bfloat16 [512, 1024], replicated, may hold values from -0.25 to 0.25
- node_out: bfloat16 [1024, 256], replicated, may hold values from -0.1875 to 0.1875
- coarse_edge_in: bfloat16 [512, 1024], replicated, may hold values from -0.25 to 0.25
- coarse_edge_out: bfloat16 [1024, 256], replicated, may hold values from -0.1875 to 0.1875
- coarse_node_in: bfloat16 [512, 1024], replicated, may hold values from -0.25 to 0.25
- coarse_node_out: bfloat16 [1024, 256], replicated, may hold values from -0.1875 to 0.1875
Outputs:
- fine_result: bfloat16 [131072, 256], P(('nodes', 'hidden'))
- edge_result: bfloat16 [131072, 6, 256], P(('nodes', 'hidden'))
- coarse_result: bfloat16 [16384, 256], P(('nodes', 'hidden'))
Inputs may be any that keep to these rules, and one draw needn't show every extreme that they name: `fine_neighbours`: -1 marks an empty slot; empty slots are the last ones of a node and at least four slots of every node are filled; every value of 128 or more that a device can receive is named by some slot of that device's nodes. `pool_send`: rows q of the sending device's 128 fine nodes, or -1; each of those rows appears exactly once in the device's lists, and filled slots of one peer come first; for each index along hidden, one device along nodes gets all 4 slots filled from every sender. `pool_recv`: at device (m, h), entry [g, s] is the coarse node, among the device's 16, of the row that device (g, h) puts in pool_send slot [m, s]; -1 exactly where that slot is -1; on every device some coarse node has no member. `coarse_neighbours`: indices among the 16 coarse nodes of the same device; -1 marks an empty slot; empty slots are the last ones and at least three are filled.
All inputs are finite; a program needn't handle non-finite values.
Results may differ from a plain program's by a relative error of at most 0.015.
Values may be sent and summed in bfloat16 or wider, within the bound.
A program may use at most 64 MiB of HBM per device.

v0:
```python
import jax
import jax.numpy as jnp
from jax import lax
from jax.sharding import PartitionSpec as P

EPSILON = 1e-05


def layer_norm(values):
    average = jnp.mean(values, axis=-1, keepdims=True)
    centred = values - average
    spread = jnp.mean(centred * centred, axis=-1, keepdims=True)
    return centred * lax.rsqrt(spread + EPSILON)


def two_layer(inputs, w_first, w_second):
    hidden_act = jnp.maximum(
        jnp.dot(inputs, w_first, preferred_element_type=jnp.float32), 0.0
    ).astype(jnp.bfloat16)
    return jnp.dot(hidden_act, w_second, preferred_element_type=jnp.float32)


def coarse_layer(
    coarse_in, neighbour_list, w_edge_first, w_edge_second, w_node_first, w_node_second
):
    row_count, latent_width = coarse_in.shape
    slot_valid = neighbour_list >= 0
    safe_index = jnp.where(slot_valid, neighbour_list, 0)
    sources = jnp.take(coarse_in, safe_index.reshape(-1), axis=0).reshape(
        row_count, -1, latent_width
    )
    sources = jnp.where(slot_valid[:, :, None], sources, jnp.zeros_like(sources))
    targets = jnp.broadcast_to(coarse_in[:, None, :], sources.shape)
    joined = jnp.concatenate([sources, targets], axis=-1).reshape(-1, 2 * latent_width)
    messages = layer_norm(two_layer(joined, w_edge_first, w_edge_second)).reshape(
        row_count, -1, latent_width
    )
    messages = jnp.where(slot_valid[:, :, None], messages, 0.0).astype(jnp.bfloat16)
    incoming = jnp.sum(messages.astype(jnp.float32), axis=1).astype(jnp.bfloat16)
    update = two_layer(jnp.concatenate([coarse_in, incoming], axis=-1), w_node_first, w_node_second)
    return (coarse_in.astype(jnp.float32) + layer_norm(update)).astype(jnp.bfloat16)


def edge_hidden(own_nodes, lookup_rows, edge_flat, safe_index, slot_valid, w_first):
    latent_width = own_nodes.shape[1]
    row_count, slot_count = safe_index.shape
    from_source = jnp.dot(
        lookup_rows, w_first[latent_width : 2 * latent_width], preferred_element_type=jnp.float32
    )
    from_target = jnp.dot(
        own_nodes, w_first[2 * latent_width :], preferred_element_type=jnp.float32
    )
    gathered = jnp.take(from_source, safe_index.reshape(-1), axis=0).reshape(
        row_count, slot_count, -1
    )
    gathered = jnp.where(slot_valid[:, :, None], gathered, 0.0)
    from_edges = jnp.dot(
        edge_flat, w_first[:latent_width], preferred_element_type=jnp.float32
    ).reshape(row_count, slot_count, -1)
    summed = from_edges + gathered + from_target[:, None, :]
    return jnp.maximum(summed, 0.0).astype(jnp.bfloat16).reshape(row_count * slot_count, -1)


def shards(
    fine_nodes,
    fine_edges,
    fine_neighbours,
    group_send,
    halo_send,
    pool_send,
    pool_recv,
    coarse_neighbours,
    edge_in,
    edge_out,
    node_in,
    node_out,
    coarse_edge_in,
    coarse_edge_out,
    coarse_node_in,
    coarse_node_out,
):
    own_count, latent_width = fine_nodes.shape
    slot_count = fine_neighbours.shape[1]
    peer_count = lax.axis_size("nodes")
    share_count = lax.axis_size("hidden")
    share_index = lax.axis_index("hidden")
    group_lists = group_send[0]
    whole_group = lax.all_gather(fine_nodes, "hidden", axis=0, tiled=True)
    wanted = lax.dynamic_index_in_dim(group_lists, share_index, 1, keepdims=False)
    group_index = (jnp.arange(share_count, dtype=jnp.int32)[:, None] * own_count + wanted).reshape(
        -1
    )
    in_group = jnp.take(whole_group, group_index, axis=0)
    outgoing = jnp.take(fine_nodes, halo_send.reshape(-1), axis=0).reshape(
        peer_count, -1, latent_width
    )
    ghosts = lax.all_to_all(outgoing, "nodes", split_axis=0, concat_axis=0, tiled=True).reshape(
        -1, latent_width
    )
    lookup_rows = jnp.concatenate([fine_nodes, in_group, ghosts], axis=0)
    slot_valid = fine_neighbours >= 0
    safe_index = jnp.where(slot_valid, fine_neighbours, 0)
    edge_flat = fine_edges.reshape(-1, latent_width)
    hidden_act = edge_hidden(fine_nodes, lookup_rows, edge_flat, safe_index, slot_valid, edge_in)
    edge_sum = jnp.dot(hidden_act, edge_out, preferred_element_type=jnp.float32)
    new_edges = jnp.where(
        slot_valid.reshape(-1, 1), edge_flat.astype(jnp.float32) + layer_norm(edge_sum), 0.0
    ).astype(jnp.bfloat16)
    new_edges = new_edges.reshape(own_count, slot_count, latent_width)
    incoming = jnp.sum(new_edges.astype(jnp.float32), axis=1).astype(jnp.bfloat16)
    update = two_layer(jnp.concatenate([fine_nodes, incoming], axis=-1), node_in, node_out)
    fine_mid = (fine_nodes.astype(jnp.float32) + layer_norm(update)).astype(jnp.bfloat16)
    chooser = (
        pool_send.reshape(-1)[:, None] == jnp.arange(own_count, dtype=jnp.int32)[None, :]
    ).astype(jnp.bfloat16)
    outgoing_pool = jnp.dot(chooser, fine_mid, preferred_element_type=jnp.float32).astype(
        jnp.bfloat16
    )
    arrived = lax.all_to_all(
        outgoing_pool.reshape(peer_count, -1, latent_width),
        "nodes",
        split_axis=0,
        concat_axis=0,
        tiled=True,
    ).reshape(-1, latent_width)
    coarse_rows = coarse_neighbours.shape[0]
    member = (
        pool_recv.reshape(-1)[None, :] == jnp.arange(coarse_rows, dtype=jnp.int32)[:, None]
    ).astype(jnp.bfloat16)
    totals = jnp.dot(member, arrived, preferred_element_type=jnp.float32)
    counts = jnp.sum(member.astype(jnp.float32), axis=1, keepdims=True)
    pooled = (totals / jnp.maximum(counts, 1.0)).astype(jnp.bfloat16)
    coarse_result = coarse_layer(
        pooled, coarse_neighbours, coarse_edge_in, coarse_edge_out, coarse_node_in, coarse_node_out
    )
    returning = jnp.dot(member.T, coarse_result, preferred_element_type=jnp.float32).astype(
        jnp.bfloat16
    )
    returned = lax.all_to_all(
        returning.reshape(peer_count, -1, latent_width),
        "nodes",
        split_axis=0,
        concat_axis=0,
        tiled=True,
    ).reshape(-1, latent_width)
    unpooled = jnp.dot(chooser.T, returned, preferred_element_type=jnp.float32)
    fine_result = (fine_mid.astype(jnp.float32) + unpooled).astype(jnp.bfloat16)
    return (fine_result, new_edges, coarse_result)


def solution(mesh):
    in_specs = (
        P(("nodes", "hidden"), None),
        P(("nodes", "hidden"), None, None),
        P(("nodes", "hidden"), None),
        P("nodes", None, None, None),
        P(("nodes", "hidden"), None, None),
        P(("nodes", "hidden"), None, None),
        P(("nodes", "hidden"), None, None),
        P(("nodes", "hidden"), None),
        P(),
        P(),
        P(),
        P(),
        P(),
        P(),
        P(),
        P(),
    )
    out_specs = (
        P(("nodes", "hidden"), None),
        P(("nodes", "hidden"), None, None),
        P(("nodes", "hidden"), None),
    )
    return jax.shard_map(shards, mesh=mesh, in_specs=in_specs, out_specs=out_specs, check_vma=False)
```

profile of v0, /device:TPU:1, one launch (start us, length us, event | category | flops | bytes accessed | tf_op | source)
XLA Modules:
  0.0 156.0 jit_solution(10612845252743119993)
XLA Ops:
  9.5 1.6 %gather_fusion.1 = bf16[128,256]{1,0:T(8,128)(2,1)S(1)} fusion(bf16[128,256]{1,0:T(8,128)(2,1)} %param.16, s32[1024]{0:T(1024)S(1)} %pad_clamp_fusion.2), kind=kCustom, calls=%fused_computation.1 | custom fusion | bytes 131584 | tf_op jit(solution)/shard_map/jit(_take)/gather | solution.py:94
  12.1 22.8 %all-to-all-start = ((bf16[64,2,256]{2,1,0:T(2,128)(2,1)}), bf16[64,2,256]{2,1,0:T(2,128)(2,1)S(1)}, u32[]{:S(2)}, u32[]{:S(2)}) async-start(bf16[64,2,256]{2,1,0:T(2,128)(2,1)} %broadcast_select_fusion), calls=%async_computation | async-start | bytes 131072 | tf_op jit(solution)/shard_map/all_to_all | solution.py:97
  34.9 1.3 dynamic-slice_reduce_fusion
  41.3 1.2 copy.42
  42.5 1.0 reshape.292
  43.9 1.3 fusion.14
  45.2 3.2 %all-to-all-done = bf16[64,2,256]{2,1,0:T(2,128)(2,1)S(1)} async-done(((bf16[64,2,256]{2,1,0:T(2,128)(2,1)}), bf16[64,2,256]{2,1,0:T(2,128)(2,1)S(1)}, u32[]{:S(2)}, u32[]{:S(2)}) %all-to-all-start) | async-done | bytes 65568 | tf_op jit(solution)/shard_map/all_to_all | solution.py:97
  48.4 17.5 %all-gather.2.cloned.1.call-done = bf16[2048,256]{1,0:T(8,128)(2,1)} async-done(((bf16[128,256]{1,0:T(8,128)(2,1)}), bf16[2048,256]{1,0:T(8,128)(2,1)}) %all-gather.2.cloned.1.call-update) | async-done | bytes 1048592 | tf_op jit(solution)/shard_map/all_gather | solution.py:88
  65.9 2.1 %gather_fusion = bf16[128,256]{1,0:T(8,128)(2,1)S(1)} fusion(bf16[2048,256]{1,0:T(8,128)(2,1)} %all-gather.2.cloned.1.call-done, s32[1024]{0:T(1024)S(1)} %pad_clamp_fusion.3), kind=kCustom, calls=%fused_computation | custom fusion | bytes 131584 | tf_op jit(solution)/shard_map/jit(_take)/gather | solution.py:93
  68.1 1.4 fusion.16
  69.5 3.6 %gather_fusion.2 = f32[768,1024]{1,0:T(8,128)} fusion(f32[384,1024]{1,0:T(8,128)S(1)} %fusion.16, s32[1024]{0:T(1024)S(1)} %pad_clamp_fusion.1), kind=kCustom, calls=%fused_computation.2 | custom fusion | bytes 6294528 | tf_op jit(solution)/shard_map/jit(_take)/gather | solution.py:53
  73.2 4.6 %gather.24 = f32[128,6,1024]{2,1,0:T(8,128)} reshape(f32[768,1024]{1,0:T(8,128)} %gather_fusion.2) | data formatting | bytes 6291456 | tf_op jit(solution)/shard_map/jit(_take)/gather | solution.py:53
  77.8 4.5 %fusion.4 = bf16[128,6,1024]{2,0,1:T(8,128)(2,1)S(1)} fusion(f32[128,6,1024]{2,1,0:T(8,128)} %gather.24, bf16[128,6,256]{2,0,1:T(8,128)(2,1)S(1)} %copy-done.6, f32[128,1024]{1,0:T(8,128)S(1)} %fusion.14, pred[128,6]{0,1:T(8,128)(4,1)S(1)} %get-tuple-element.13, pred[128,6]{0,1:T(8,128)(4,1)S(1)} %get-tuple-element.12, bf16[768,1024]{1,0:T(8,128)(2,1)} %param.24), kind=kOutput, calls=%fused_computation.9 | convolution fusion | flops 407371776 | bytes 7210496 | tf_op jit(solution)/shard_map/dot_general | solution.py:57
  82.4 0.9 copy.47
  83.3 1.5 reshape.283
  84.7 2.2 %fusion.65 = (f32[768]{0:T(1024)S(1)}, f32[768,256]{1,0:T(8,128)S(1)}) fusion(bf16[768,1024]{1,0:T(8,128)(2,1)} %reshape.283, bf16[1024,256]{1,0:T(8,128)(2,1)} %param.25), kind=kOutput, calls=%fused_computation.111 | convolution fusion | flops 402849024 | bytes 2886656 | tf_op jit(solution)/shard_map/dot_general | solution.py:105
  90.0 16.3 %all-to-all-start.1 = ((bf16[64,4,256]{2,1,0:T(4,128)(2,1)}), bf16[64,4,256]{2,1,0:T(4,128)(2,1)S(1)}, u32[]{:S(2)}, u32[]{:S(2)}) async-start(bf16[64,4,256]{2,1,0:T(4,128)(2,1)} %reshape.285), calls=%async_computation.1 | async-start | bytes 262144 | tf_op jit(solution)/shard_map/all_to_all | solution.py:119
  106.4 14.3 %all-to-all-done.1 = bf16[64,4,256]{2,1,0:T(4,128)(2,1)S(1)} async-done(((bf16[64,4,256]{2,1,0:T(4,128)(2,1)}), bf16[64,4,256]{2,1,0:T(4,128)(2,1)S(1)}, u32[]{:S(2)}, u32[]{:S(2)}) %all-to-all-start.1) | async-done | bytes 131104 | tf_op jit(solution)/shard_map/all_to_all | solution.py:119
  121.8 1.6 %fusion.69 = (f32[96]{0:T(128)S(1)}, f32[96,256]{1,0:T(8,128)S(1)}) fusion(bf16[1024,256]{1,0:T(8,128)(2,1)} %param.29, bf16[512,1024]{1,0:T(8,128)(2,1)S(1)} %copy-done.3, bf16[96,256]{1,0:T(8,128)(2,1)S(1)} %concatenate.17, bf16[96,256]{1,0:T(8,128)(2,1)S(1)} %select_select_fusion), kind=kOutput, calls=%fused_computation.113 | convolution fusion | flops 151412640 | bytes 1769856 | tf_op jit(solution)/shard_map/dot_general | solution.py:20
  123.9 1.8 %fusion.72 = (f32[16]{0:T(128)S(1)}, f32[16,256]{1,0:T(8,128)S(1)}) fusion(bf16[1024,256]{1,0:T(8,128)(2,1)S(1)} %copy-done.4, bf16[512,1024]{1,0:T(8,128)(2,1)} %param.30, bf16[16,256]{1,0:T(8,128)(2,1)S(1)} %fusion.38, bf16[16,256]{1,0:T(8,128)(2,1)S(1)} %fusion.12), kind=kOutput, calls=%fused_computation.114 | convolution fusion | flops 25235440 | bytes 1605696 | tf_op jit(solution)/shard_map/dot_general | solution.py:20
  126.9 7.2 %all-to-all-start.2 = ((bf16[64,4,256]{2,1,0:T(4,128)(2,1)}), bf16[64,4,256]{2,1,0:T(4,128)(2,1)S(1)}, u32[]{:S(2)}, u32[]{:S(2)}) async-start(bf16[64,4,256]{2,1,0:T(4,128)(2,1)} %reshape.290), calls=%async_computation.2 | async-start | bytes 262144 | tf_op jit(solution)/shard_map/all_to_all | solution.py:139
  134.1 0.8 copy.54
  134.9 13.2 %all-to-all-done.2 = bf16[64,4,256]{2,1,0:T(4,128)(2,1)S(1)} async-done(((bf16[64,4,256]{2,1,0:T(4,128)(2,1)}), bf16[64,4,256]{2,1,0:T(4,128)(2,1)S(1)}, u32[]{:S(2)}, u32[]{:S(2)}) %all-to-all-start.2) | async-done | bytes 131104 | tf_op jit(solution)/shard_map/all_to_all | solution.py:139
  148.2 0.9 fusion.9
  (95 shorter events, 14.6 us)
Async XLA Ops:
  7.2 81.0 %copy-start = (bf16[512,1024]{1,0:T(8,128)(2,1)S(1)}, bf16[512,1024]{1,0:T(8,128)(2,1)}, u32[]{:S(2)}) copy-start(bf16[512,1024]{1,0:T(8,128)(2,1)} %param.26) | copy-start | bytes 3145732
  7.2 58.7 %all-gather.2.cloned.1.call-start = ((), (), s32[]{:S(2)}) async-start(), calls=%async_computation.3 | async-start | bytes 1114112 | tf_op jit(solution)/shard_map/all_gather | solution.py:88
  11.1 32.4 %copy-start.8 = (s32[1,64,4]{1,2,0:T(4,128)S(1)}, s32[1,64,4]{1,2,0:T(4,128)}, u32[]{:S(2)}) copy-start(s32[1,64,4]{1,2,0:T(4,128)} %param.21) | copy-start | bytes 3076
  11.2 32.8 %copy-start.1 = (bf16[128,256]{1,0:T(8,128)(2,1)S(1)}, bf16[128,256]{1,0:T(8,128)(2,1)}, u32[]{:S(2)}) copy-start(bf16[128,256]{1,0:T(8,128)(2,1)} %param.16) | copy-start | bytes 196612
  12.1 36.3 %all-to-all-start = ((bf16[64,2,256]{2,1,0:T(2,128)(2,1)}), bf16[64,2,256]{2,1,0:T(2,128)(2,1)S(1)}, u32[]{:S(2)}, u32[]{:S(2)}) async-start(bf16[64,2,256]{2,1,0:T(2,128)(2,1)} %broadcast_select_fusion), calls=%async_computation | async-start | bytes 131072 | tf_op jit(solution)/shard_map/all_to_all | solution.py:97
  73.2 4.6 %copy-start.6 = (bf16[128,6,256]{2,0,1:T(8,128)(2,1)S(1)}, bf16[128,6,256]{2,0,1:T(8,128)(2,1)}, u32[]{:S(2)}) copy-start(bf16[128,6,256]{2,0,1:T(8,128)(2,1)} %param.17) | copy-start | bytes 1179652
  84.7 2.6 %copy-start.2 = (f32[768,256]{1,0:T(8,128)S(1)}, f32[768,256]{1,0:T(8,128)}, u32[]{:S(2)}) copy-start(f32[768,256]{1,0:T(8,128)} %reshape.292) | copy-start | bytes 2359300
  87.0 1.2 copy-start.5
  88.2 33.6 %copy-start.3 = (bf16[512,1024]{1,0:T(8,128)(2,1)S(1)}, bf16[512,1024]{1,0:T(8,128)(2,1)}, u32[]{:S(2)}) copy-start(bf16[512,1024]{1,0:T(8,128)(2,1)} %param.28) | copy-start | bytes 3145732
  89.1 34.9 %copy-start.4 = (bf16[1024,256]{1,0:T(8,128)(2,1)S(1)}, bf16[1024,256]{1,0:T(8,128)(2,1)}, u32[]{:S(2)}) copy-start(bf16[1024,256]{1,0:T(8,128)(2,1)} %param.31) | copy-start | bytes 1572868
  90.0 30.7 %all-to-all-start.1 = ((bf16[64,4,256]{2,1,0:T(4,128)(2,1)}), bf16[64,4,256]{2,1,0:T(4,128)(2,1)S(1)}, u32[]{:S(2)}, u32[]{:S(2)}) async-start(bf16[64,4,256]{2,1,0:T(4,128)(2,1)} %reshape.285), calls=%async_computation.1 | async-start | bytes 262144 | tf_op jit(solution)/shard_map/all_to_all | solution.py:119
  126.0 23.1 %copy-start.7 = (bf16[16,256]{1,0:T(8,128)(2,1)}, bf16[16,256]{1,0:T(8,128)(2,1)S(1)}, u32[]{:S(2)}) copy-start(bf16[16,256]{1,0:T(8,128)(2,1)S(1)} %add_convert_fusion.1) | copy-start | bytes 24580
  126.9 21.2 %all-to-all-start.2 = ((bf16[64,4,256]{2,1,0:T(4,128)(2,1)}), bf16[64,4,256]{2,1,0:T(4,128)(2,1)S(1)}, u32[]{:S(2)}, u32[]{:S(2)}) async-start(bf16[64,4,256]{2,1,0:T(4,128)(2,1)} %reshape.290), calls=%async_computation.2 | async-start | bytes 262144 | tf_op jit(solution)/shard_map/all_to_all | solution.py:139
Sparse Core Ops, SparseCore 0:
  10.7 55.1 all-gather.1
where the time goes:
time: 158 us; the launch traced here: 156 us
  waiting for transfers between devices  48.9 us (31%)
  starting transfers between devices  46.3 us (29%)
  local copies, waits for them, and re-layouts  24.7 us (16%)
  matrix products  14.9 us (9%)
  between operations  14.5 us (9%)
  other arithmetic  6.6 us (4%)
    all_to_all x1, starting transfers between devices, shards(): lax.all_to_all(outgoing, 'nodes', split_axis=0, concat_axis=0, tiled=True)  22.8 us
    all_gather x1, waiting for transfers between devices, shards(): whole_group = lax.all_gather(fine_nodes, 'hidden', axis=0, tiled=True)  17.5 us
    all_to_all x1, starting transfers between devices, shards(): lax.all_to_all(outgoing_pool.reshape(peer_count, -1, latent_width), 'node...  16.3 us
    all_to_all x1, waiting for transfers between devices, shards(): lax.all_to_all(outgoing_pool.reshape(peer_count, -1, latent_width), 'node...  14.3 us
    all_to_all x1, waiting for transfers between devices, shards(): lax.all_to_all(returning.reshape(peer_count, -1, latent_width), 'nodes',...  13.2 us
    gather x2, local copies, waits for them, and re-layouts, edge_hidden(): jnp.take(from_source, safe_index.reshape(-1), axis=0)  8.29 us
    all_to_all x1, starting transfers between devices, shards(): lax.all_to_all(returning.reshape(peer_count, -1, latent_width), 'nodes',...  7.16 us
    dot_general x1, matrix products, edge_hidden(): jnp.dot(edge_flat, w_first[:latent_width], preferred_element_type=jnp.flo...  4.52 us
  transfers between devices with their start and end apart: 4, of which 4 were waited for; matrix products, arithmetic and copies ran while one was open for 10% of the time, Pallas kernels for 0%

commit v1 on v0

v1 whole, which is shorter than its diff:
```python
import jax
import jax.numpy as jnp
from jax import lax
from jax.experimental import pallas as pl
from jax.experimental.pallas import tpu as pltpu
from jax.sharding import PartitionSpec as P

EPSILON = 1e-05
MESH = pl.DeviceIdType.MESH
BF16 = jnp.bfloat16
F32 = jnp.float32
NX, NZ = 4, 16
NODES, HIDDEN = NX * NZ, 16
ROWS, WIDTH, UNITS = 128, 256, 1024
SLOTS = 6
EDGES = ROWS * SLOTS
COARSE = 16
COARSE_EDGES = COARSE * SLOTS
MSG = NODES * 8


def dot(a, b):
    return jnp.dot(a, b, preferred_element_type=F32)


def dot_nt(a, b):
    return lax.dot_general(a, b, (((1,), (1,)), ((), ())), preferred_element_type=F32)


def layer_norm(values):
    average = jnp.mean(values, axis=-1, keepdims=True)
    centred = values - average
    spread = jnp.mean(centred * centred, axis=-1, keepdims=True)
    return centred * lax.rsqrt(spread + EPSILON)


def iota(shape, dim):
    return lax.broadcasted_iota(jnp.int32, shape, dim)


def one_hot(condition):
    return jnp.where(condition, 1.0, 0.0).astype(BF16)


def spread_column(lists, rows, shift):
    slots, peers = lists.shape
    pick_peer = one_hot((iota((rows, peers), 0) >> shift) == iota((rows, peers), 1))
    table = dot_nt(pick_peer, lists.astype(F32).astype(BF16))
    slot = (iota((rows, slots), 0) & ((1 << shift) - 1)) >> 1
    return jnp.sum(
        jnp.where(slot == iota((rows, slots), 1), table, 0.0), axis=1, keepdims=True
    ).astype(jnp.int32)


def spread_row(lists, rows, shift):
    slots, peers = lists.shape
    pick_peer = one_hot((iota((peers, rows), 1) >> shift) == iota((peers, rows), 0))
    table = dot(lists.astype(F32).astype(BF16), pick_peer)
    slot = (iota((slots, rows), 1) & ((1 << shift) - 1)) >> 1
    return jnp.sum(
        jnp.where(slot == iota((slots, rows), 0), table, 0.0), axis=0, keepdims=True
    ).astype(jnp.int32)


def halves(rows):
    return jnp.concatenate([rows[:, :128], rows[:, 128:]], axis=0)


def row_picker(column):
    shape = (column.shape[0], 2 * ROWS)
    lane = iota(shape, 1)
    return one_hot((column == (lane & 127)) & ((iota(shape, 0) & 1) == (lane >> 7)))


def kernel(
    nodes_hbm, edges_hbm, neigh_hbm, group_hbm, halo_hbm, psend_hbm, precv_hbm, cneigh_hbm,
    w_ei_hbm, w_eo_hbm, w_ni_hbm, w_no_hbm, w_cei_hbm, w_ceo_hbm, w_cni_hbm, w_cno_hbm,
    fine_out, edge_out, coarse_out,
    nodes, edges, neigh, group, halo, psend, precv, cneigh,
    w_ei, w_eo, w_ni, w_no, w_cei, w_ceo, w_cni, w_cno,
    first_part, new_edges,
    group_src, group_dst, ghost_src, ghost_dst, pool_src, pool_dst, back_src, back_dst,
    load_sems, store_sem, send_sems, recv_sems,
):
    node_at = lax.axis_index("nodes")
    hidden_at = lax.axis_index("hidden")
    x_at = lax.div(node_at, NZ)
    z_at = lax.rem(node_at, NZ)

    barrier = pltpu.get_barrier_semaphore()

    def far_first(visit):
        def step(t, carry):
            away = (t + 1) >> 1
            dz = NZ // 2 + away * (1 - 2 * (t & 1))
            for dx in (2, 1, 3, 0):
                visit(lax.rem(x_at + dx, NX) * NZ + lax.rem(z_at + dz, NZ))
            return carry

        lax.fori_loop(0, NZ - 1, step, 0)
        for dx in (2, 1, 3):
            visit(lax.rem(x_at + dx, NX) * NZ + z_at)

    def group_first(visit):
        def step(t, carry):
            visit(lax.rem(hidden_at + t, HIDDEN))
            return carry

        lax.fori_loop(1, HIDDEN, step, 0)

    far_first(
        lambda p: pl.semaphore_signal(barrier, inc=1, device_id={"nodes": p}, device_id_type=MESH)
    )
    group_first(
        lambda p: pl.semaphore_signal(barrier, inc=1, device_id={"hidden": p}, device_id_type=MESH)
    )

    loads = []
    sources = (
        nodes_hbm, group_hbm.at[0, hidden_at], halo_hbm, psend_hbm, precv_hbm, neigh_hbm, cneigh_hbm,
        w_ei_hbm, edges_hbm, w_eo_hbm, w_ni_hbm, w_no_hbm, w_cei_hbm, w_ceo_hbm, w_cni_hbm, w_cno_hbm,
    )
    targets = (
        nodes, group, halo, psend, precv, neigh, cneigh,
        w_ei, edges, w_eo, w_ni, w_no, w_cei, w_ceo, w_cni, w_cno,
    )
    for i, (source, target) in enumerate(zip(sources, targets)):
        copy = pltpu.make_async_copy(source, target, load_sems.at[i])
        copy.start()
        loads.append(copy)

    for i in range(3):
        loads[i].wait()
    own = nodes[...]
    own_halves = halves(own)
    group_pick = row_picker(spread_column(group[...], HIDDEN * 16, 4))
    group_src[...] = dot(group_pick, own_halves).astype(BF16).reshape(HIDDEN, 16, 128)
    ghost_pick = row_picker(spread_column(halo[0], MSG, 3))
    ghost_src[...] = dot(ghost_pick, own_halves).reshape(NODES, 8, 128).astype(BF16)

    pl.semaphore_wait(barrier, NODES - 1 + HIDDEN - 1)

    def send(src, dst, which):
        def visit(p):
            pltpu.make_async_remote_copy(
                src_ref=src.at[p],
                dst_ref=dst.at[node_at],
                send_sem=send_sems.at[which],
                recv_sem=recv_sems.at[which],
                device_id={"nodes": p},
                device_id_type=MESH,
            ).start()

        far_first(visit)

    def send_group(p):
        pltpu.make_async_remote_copy(
            src_ref=group_src.at[p],
            dst_ref=group_dst.at[hidden_at],
            send_sem=send_sems.at[0],
            recv_sem=recv_sems.at[0],
            device_id={"hidden": p},
            device_id_type=MESH,
        ).start()

    def wait_all(buffer, count, sem):
        pltpu.make_async_copy(buffer.at[pl.ds(0, count)], buffer.at[pl.ds(0, count)], sem).wait()

    send(ghost_src, ghost_dst, 1)
    group_first(send_group)

    for i in range(3, 7):
        loads[i].wait()
    lists = jnp.concatenate(
        [neigh[...].astype(F32), jnp.zeros((ROWS - SLOTS, ROWS), F32)], axis=0
    )
    neigh_columns = lists.T.astype(jnp.int32)
    column = jnp.concatenate([neigh_columns[:, k : k + 1] for k in range(SLOTS)], axis=0)
    lane = iota((EDGES, ROWS), 1)
    take_own = one_hot(column == lane)
    take_group = one_hot(column == lane + ROWS)
    take_ghost = one_hot(column == lane + 2 * ROWS)
    valid = column >= 0

    send_column = spread_column(psend[0], MSG, 3)
    send_row = spread_row(psend[0], MSG, 3)
    pool_pick = row_picker(send_column)
    shape = (2 * ROWS, MSG)
    sub = iota(shape, 0)
    back_pick = one_hot((send_row == (sub & 127)) & ((iota(shape, 1) & 1) == (sub >> 7)))
    recv_column = spread_column(precv[0], MSG, 3)
    recv_row = spread_row(precv[0], MSG, 3)
    shape = (2 * COARSE, MSG)
    sub = iota(shape, 0)
    member = one_hot((recv_row == (sub & 15)) & ((iota(shape, 1) & 1) == (sub >> 4)))
    shape = (MSG, 2 * COARSE)
    lane = iota(shape, 1)
    member_back = one_hot((recv_column == (lane & 15)) & ((iota(shape, 0) & 1) == (lane >> 4)))
    counts = jnp.sum(member[:COARSE].astype(F32), axis=1, keepdims=True)
    scale_down = jnp.maximum(counts, 1.0)

    lists = jnp.concatenate(
        [cneigh[...].astype(F32), jnp.zeros((8 - SLOTS, COARSE), F32)], axis=0
    )
    lists = jnp.concatenate([lists, jnp.zeros((8, 128 - COARSE), F32)], axis=1)
    lists = jnp.concatenate([lists, jnp.zeros((120, 128), F32)], axis=0)
    coarse_columns = lists.T[:COARSE].astype(jnp.int32)
    coarse_column = jnp.concatenate(
        [coarse_columns[:, k : k + 1] for k in range(SLOTS)], axis=0
    )
    take_coarse = one_hot(coarse_column == iota((COARSE_EDGES, COARSE), 1))
    coarse_valid = coarse_column >= 0

    def half_of(shape, half, shift, slot_bits):
        row = iota(shape, 0)
        lane = iota(shape, 1)
        wanted = ((row >> slot_bits) << shift) + ((row & ((1 << slot_bits) - 1)) << 1) + half
        return one_hot(lane == wanted)

    group_split = [half_of((ROWS, HIDDEN * 16), half, 4, 3) for half in range(2)]
    ghost_split = [half_of((ROWS, MSG), half, 3, 1) for half in range(2)]

    loads[7].wait()
    loads[8].wait()
    from_target = dot(own, w_ei[2 * WIDTH :, :])
    for k in range(SLOTS):
        rows = pl.ds(k * ROWS, ROWS)
        first_part[rows, :] = dot(edges[rows, :], w_ei[:WIDTH, :]) + from_target
    for i in range(9, 16):
        loads[i].wait()
    node_part = dot(own, w_ni[:WIDTH, :])
    from_own = dot(take_own, own)

    group_dst[pl.ds(hidden_at, 1)] = group_src[pl.ds(hidden_at, 1)]
    wait_all(group_dst, HIDDEN - 1, recv_sems.at[0])
    arrived = group_dst[...].reshape(HIDDEN * 16, 128)
    in_group = jnp.concatenate([dot(split, arrived) for split in group_split], axis=1).astype(BF16)
    from_near = from_own + dot(take_group, in_group)

    ghost_dst[pl.ds(node_at, 1)] = ghost_src[pl.ds(node_at, 1)]
    wait_all(ghost_dst, NODES - 1, recv_sems.at[1])

    def flat(buffer):
        return buffer[...].astype(F32).reshape(MSG, 128).astype(BF16)

    arrived = flat(ghost_dst)
    ghosts = jnp.concatenate([dot(split, arrived) for split in ghost_split], axis=1).astype(BF16)
    source = (from_near + dot(take_ghost, ghosts)).astype(BF16)
    total = None
    for c in range(0, UNITS, WIDTH):
        hidden = first_part[:, c : c + WIDTH] + dot(source, w_ei[WIDTH : 2 * WIDTH, c : c + WIDTH])
        part = dot(jnp.maximum(hidden, 0.0).astype(BF16), w_eo[c : c + WIDTH, :])
        total = part if total is None else total + part
    result = jnp.where(valid, edges[...].astype(F32) + layer_norm(total), 0.0).astype(BF16)
    new_edges[...] = result
    store = pltpu.make_async_copy(new_edges, edge_out, store_sem)
    store.start()
    incoming = None
    for k in range(SLOTS):
        part = result[k * ROWS : (k + 1) * ROWS].astype(F32)
        incoming = part if incoming is None else incoming + part
    incoming = incoming.astype(BF16)
    hidden = jnp.maximum(node_part + dot(incoming, w_ni[WIDTH:, :]), 0.0).astype(BF16)
    fine_mid = (own.astype(F32) + layer_norm(dot(hidden, w_no[...]))).astype(BF16)

    pool_src[...] = dot(pool_pick, halves(fine_mid)).reshape(NODES, 8, 128).astype(BF16)
    send(pool_src, pool_dst, 2)
    pool_dst[pl.ds(node_at, 1)] = pool_src[pl.ds(node_at, 1)]
    wait_all(pool_dst, NODES - 1, recv_sems.at[2])

    sums = dot(member, flat(pool_dst))
    pooled = jnp.concatenate([sums[:COARSE], sums[COARSE:]], axis=1) / scale_down
    pooled = pooled.astype(BF16)
    from_target = dot(pooled, w_cei[WIDTH:, :])
    source = dot(take_coarse, pooled).astype(BF16)
    hidden = dot(source, w_cei[:WIDTH, :]) + jnp.concatenate([from_target] * SLOTS, axis=0)
    hidden = jnp.maximum(hidden, 0.0).astype(BF16)
    messages = jnp.where(coarse_valid, layer_norm(dot(hidden, w_ceo[...])), 0.0).astype(BF16)
    incoming = None
    for k in range(SLOTS):
        part = messages[k * COARSE : (k + 1) * COARSE].astype(F32)
        incoming = part if incoming is None else incoming + part
    incoming = incoming.astype(BF16)
    hidden = dot(pooled, w_cni[:WIDTH, :]) + dot(incoming, w_cni[WIDTH:, :])
    hidden = jnp.maximum(hidden, 0.0).astype(BF16)
    coarse = (pooled.astype(F32) + layer_norm(dot(hidden, w_cno[...]))).astype(BF16)
    coarse_out[...] = coarse

    back_src[...] = dot(member_back, halves(coarse)).reshape(NODES, 8, 128).astype(BF16)
    send(back_src, back_dst, 3)
    back_dst[pl.ds(node_at, 1)] = back_src[pl.ds(node_at, 1)]
    wait_all(back_dst, NODES - 1, recv_sems.at[3])

    returned = dot(back_pick, flat(back_dst))
    unpooled = jnp.concatenate([returned[:ROWS], returned[ROWS:]], axis=1)
    fine_out[...] = (fine_mid.astype(F32) + unpooled).astype(BF16)

    store.wait()
    wait_all(group_dst, HIDDEN - 1, send_sems.at[0])
    for which, buffer in ((1, ghost_dst), (2, pool_dst), (3, back_dst)):
        wait_all(buffer, NODES - 1, send_sems.at[which])


def shards(
    fine_nodes, fine_edges, fine_neighbours, group_send, halo_send, pool_send, pool_recv,
    coarse_neighbours, *weights,
):
    anywhere = pl.BlockSpec(memory_space=pl.ANY)
    in_vmem = pl.BlockSpec(memory_space=pltpu.VMEM)
    operands = (
        fine_nodes,
        fine_edges.transpose(1, 0, 2).reshape(EDGES, WIDTH),
        fine_neighbours.T,
        group_send.transpose(0, 1, 3, 2),
        halo_send.transpose(0, 2, 1),
        pool_send.transpose(0, 2, 1),
        pool_recv.transpose(0, 2, 1),
        coarse_neighbours.T,
    ) + weights
    message = pltpu.VMEM((NODES, 8, 128), BF16)
    group_message = pltpu.VMEM((HIDDEN, 16, 128), BF16)
    fine_result, edge_result, coarse_result = pl.pallas_call(
        kernel,
        out_shape=(
            jax.ShapeDtypeStruct((ROWS, WIDTH), BF16),
            jax.ShapeDtypeStruct((EDGES, WIDTH), BF16),
            jax.ShapeDtypeStruct((COARSE, WIDTH), BF16),
        ),
        in_specs=[anywhere] * len(operands),
        out_specs=(in_vmem, anywhere, in_vmem),
        scratch_shapes=[
            pltpu.VMEM((ROWS, WIDTH), BF16),
            pltpu.VMEM((EDGES, WIDTH), BF16),
            pltpu.VMEM((SLOTS, ROWS), jnp.int32),
            pltpu.VMEM((8, HIDDEN), jnp.int32),
            pltpu.VMEM((1, 2, NODES), jnp.int32),
            pltpu.VMEM((1, 4, NODES), jnp.int32),
            pltpu.VMEM((1, 4, NODES), jnp.int32),
            pltpu.VMEM((SLOTS, COARSE), jnp.int32),
        ]
        + [pltpu.VMEM(w.shape, BF16) for w in weights]
        + [
            pltpu.VMEM((EDGES, UNITS), F32),
            pltpu.VMEM((EDGES, WIDTH), BF16),
            group_message, group_message,
            message, message, message, message, message, message,
            pltpu.SemaphoreType.DMA((16,)),
            pltpu.SemaphoreType.DMA,
            pltpu.SemaphoreType.DMA((4,)),
            pltpu.SemaphoreType.DMA((4,)),
        ],
        compiler_params=pltpu.CompilerParams(
            collective_id=0, has_side_effects=True, vmem_limit_bytes=56 * 1024 * 1024
        ),
        cost_estimate=pl.CostEstimate(
            flops=2_100_000_000, bytes_accessed=8_000_000, transcendentals=2000
        ),
    )(*operands)
    edge_result = edge_result.reshape(SLOTS, ROWS, WIDTH).transpose(1, 0, 2)
    return fine_result, edge_result, coarse_result


def solution(mesh):
    rows = ("nodes", "hidden")
    in_specs = (
        P(rows, None),
        P(rows, None, None),
        P(rows, None),
        P("nodes", None, None, None),
        P(rows, None, None),
        P(rows, None, None),
        P(rows, None, None),
        P(rows, None),
    ) + (P(),) * 8
    out_specs = (P(rows, None), P(rows, None, None), P(rows, None))
    return jax.shard_map(shards, mesh=mesh, in_specs=in_specs, out_specs=out_specs, check_vma=False)
```

time: 158 us -> 62 us (0.39)
  Pallas kernels: 0 us -> 56.2 us
  waiting for transfers between devices: 48.9 us -> 0 us
  starting transfers between devices: 46.3 us -> 0 us
  local copies, waits for them, and re-layouts: 24.7 us -> 4.53 us
  matrix products: 14.9 us -> 0 us
  between operations: 14.5 us -> 0.65 us
  other arithmetic: 6.6 us -> 0 us
    pallas_call x0 -> x1, Pallas kernels: none -> 56.2 us  [shards(): pl.pallas_call(kernel, out_shape=(jax.ShapeDtypeStruct((ROWS, WIDTH), BF1...]
    all_to_all x3 -> x0, starting transfers between devices: 46.3 us -> none  [the longest x1 22.8 us: shards(): lax.all_to_all(outgoing, 'nodes', split_axis=0, concat_axis=0, tiled=True)]
    all_to_all x3 -> x0, waiting for transfers between devices: 30.8 us -> none  [the longest x1 14.3 us: shards(): lax.all_to_all(outgoing_pool.reshape(peer_count, -1, latent_width), 'node...]
    all_gather x1 -> x0, waiting for transfers between devices: 17.5 us -> none  [shards(): whole_group = lax.all_gather(fine_nodes, 'hidden', axis=0, tiled=True)]
    dot_general x11 -> x0, matrix products: 14.9 us -> none  [the longest x1 4.52 us: edge_hidden(): jnp.dot(edge_flat, w_first[:latent_width], preferred_element_type=jnp.flo...]
    gather x6 -> x0, local copies, waits for them, and re-layouts: 12.8 us -> none  [the longest x2 8.29 us: edge_hidden(): jnp.take(from_source, safe_index.reshape(-1), axis=0)]
    reshape x12 -> x0, local copies, waits for them, and re-layouts: 3.54 us -> none  [the longest x1 1.45 us: edge_hidden(): jnp.maximum(summed, 0.0).astype(jnp.bfloat16)]
    convert_element_type x3 -> x0, local copies, waits for them, and re-layouts: 3.11 us -> none  [the longest x2 2.23 us: shards(): edge_flat.astype(jnp.float32) + layer_norm(edge_sum)]
  transfers between devices with their start and end apart: 4 -> 0, of which waited for: 4 -> 0; matrix products, arithmetic and copies ran while one was open for 10% -> 0% of each run, Pallas kernels for 0% -> 0%
where the time goes in v1:
time: 62 us; the launch traced here: 61.4 us
  Pallas kernels  56.2 us (91%)
  local copies, waits for them, and re-layouts  4.53 us (7%)
  between operations  0.65 us (1%)
    pallas_call x1, Pallas kernels, shards(): pl.pallas_call(kernel, out_shape=(jax.ShapeDtypeStruct((ROWS, WIDTH), BF1...  56.2 us
    unnamed x3, local copies, waits for them, and re-layouts  4.53 us

profile of v1, /device:TPU:1, one launch (start us, length us, event | category | flops | bytes accessed | tf_op | source)
XLA Modules:
  0.0 61.4 jit_solution(7718472714454767164)
XLA Ops:
  0.6 56.2 %shard_map.175 = (bf16[128,256]{1,0:T(8,128)(2,1)}, bf16[768,256]{1,0:T(8,128)(2,1)}, bf16[16,256]{1,0:T(8,128)(2,1)}) custom-call(bf16[128,256]{1,0:T(8,128)(2,1)} %nodes_hbm.1, bf16[768,256]{1,0:T(8,128)(2,1)} %bitcast.13, s32[6,128]{1,0:T(8,128)} %bitcast.15, s32[1,16,8,16]{3,2,1,0:T(8,128)} %bitcast.14, s32[1,2,64]{2,1,0:T(2,128)} %bitcast.19, ...), custom_call_target="tpu_custom_call" | custom-call | flops 2100000000 | bytes 8000000 | tf_op jit(solution)/shard_map/pallas_call | solution.py:322
  56.8 1.5 %copy.22 = bf16[128,256]{1,0:T(8,128)(2,1)} copy(bf16[128,256]{1,0:T(8,128)(2,1)} %get-tuple-element.12) | data formatting | bytes 131072
  58.3 1.8 %copy.23 = bf16[128,6,256]{2,0,1:T(8,128)(2,1)} copy(bf16[128,6,256]{2,0,1:T(8,128)(2,1)} %bitcast.12) | data formatting | bytes 786432
  60.1 1.3 %copy.24 = bf16[16,256]{1,0:T(8,128)(2,1)} copy(bf16[16,256]{1,0:T(8,128)(2,1)} %get-tuple-element.14) | data formatting | bytes 16384

commit v2 on v1

--- a/solution.py
+++ b/solution.py
@@ -78,9 +78,9 @@
     fine_out, edge_out, coarse_out,
     nodes, edges, neigh, group, halo, psend, precv, cneigh,
     w_ei, w_eo, w_ni, w_no, w_cei, w_ceo, w_cni, w_cno,
-    first_part, new_edges,
+    first_part,
     group_src, group_dst, ghost_src, ghost_dst, pool_src, pool_dst, back_src, back_dst,
-    load_sems, store_sem, send_sems, recv_sems,
+    load_sems, send_sems, recv_sems,
 ):
     node_at = lax.axis_index("nodes")
     hidden_at = lax.axis_index("hidden")
@@ -136,7 +136,7 @@
     group_pick = row_picker(spread_column(group[...], HIDDEN * 16, 4))
     group_src[...] = dot(group_pick, own_halves).astype(BF16).reshape(HIDDEN, 16, 128)
     ghost_pick = row_picker(spread_column(halo[0], MSG, 3))
-    ghost_src[...] = dot(ghost_pick, own_halves).reshape(NODES, 8, 128).astype(BF16)
+    ghost_src[...] = dot(ghost_pick, own_halves).reshape(NODES, 8, 128)[:, :4].astype(BF16)
 
     pl.semaphore_wait(barrier, NODES - 1 + HIDDEN - 1)
 
@@ -243,7 +243,9 @@
     def flat(buffer):
         return buffer[...].astype(F32).reshape(MSG, 128).astype(BF16)
 
-    arrived = flat(ghost_dst)
+    arrived = ghost_dst[...].astype(F32)
+    arrived = jnp.concatenate([arrived, jnp.zeros_like(arrived)], axis=1)
+    arrived = arrived.reshape(MSG, 128).astype(BF16)
     ghosts = jnp.concatenate([dot(split, arrived) for split in ghost_split], axis=1).astype(BF16)
     source = (from_near + dot(take_ghost, ghosts)).astype(BF16)
     total = None
@@ -252,9 +254,7 @@
         part = dot(jnp.maximum(hidden, 0.0).astype(BF16), w_eo[c : c + WIDTH, :])
         total = part if total is None else total + part
     result = jnp.where(valid, edges[...].astype(F32) + layer_norm(total), 0.0).astype(BF16)
-    new_edges[...] = result
-    store = pltpu.make_async_copy(new_edges, edge_out, store_sem)
-    store.start()
+    edge_out[...] = result
     incoming = None
     for k in range(SLOTS):
         part = result[k * ROWS : (k + 1) * ROWS].astype(F32)
@@ -295,10 +295,18 @@
     unpooled = jnp.concatenate([returned[:ROWS], returned[ROWS:]], axis=1)
     fine_out[...] = (fine_mid.astype(F32) + unpooled).astype(BF16)
 
-    store.wait()
     wait_all(group_dst, HIDDEN - 1, send_sems.at[0])
     for which, buffer in ((1, ghost_dst), (2, pool_dst), (3, back_dst)):
         wait_all(buffer, NODES - 1, send_sems.at[which])
+
+
+def hand_over(*refs):
+    sems = refs[-1]
+    copies = [pltpu.make_async_copy(refs[i], refs[3 + i], sems.at[i]) for i in range(3)]
+    for copy in copies:
+        copy.start()
+    for copy in copies:
+        copy.wait()
 
 
 def shards(
@@ -319,15 +327,16 @@
     ) + weights
     message = pltpu.VMEM((NODES, 8, 128), BF16)
     group_message = pltpu.VMEM((HIDDEN, 16, 128), BF16)
-    fine_result, edge_result, coarse_result = pl.pallas_call(
+    results = (
+        jax.ShapeDtypeStruct((ROWS, WIDTH), BF16),
+        jax.ShapeDtypeStruct((EDGES, WIDTH), BF16),
+        jax.ShapeDtypeStruct((COARSE, WIDTH), BF16),
+    )
+    held = pl.pallas_call(
         kernel,
-        out_shape=(
-            jax.ShapeDtypeStruct((ROWS, WIDTH), BF16),
-            jax.ShapeDtypeStruct((EDGES, WIDTH), BF16),
-            jax.ShapeDtypeStruct((COARSE, WIDTH), BF16),
-        ),
+        out_shape=tuple(pltpu.VMEM(r.shape, BF16) for r in results),
         in_specs=[anywhere] * len(operands),
-        out_specs=(in_vmem, anywhere, in_vmem),
+        out_specs=(in_vmem,) * 3,
         scratch_shapes=[
             pltpu.VMEM((ROWS, WIDTH), BF16),
             pltpu.VMEM((EDGES, WIDTH), BF16),
@@ -341,11 +350,10 @@
         + [pltpu.VMEM(w.shape, BF16) for w in weights]
         + [
             pltpu.VMEM((EDGES, UNITS), F32),
-            pltpu.VMEM((EDGES, WIDTH), BF16),
             group_message, group_message,
-            message, message, message, message, message, message,
+            pltpu.VMEM((NODES, 4, 128), BF16), pltpu.VMEM((NODES, 4, 128), BF16),
+            message, message, message, message,
             pltpu.SemaphoreType.DMA((16,)),
-            pltpu.SemaphoreType.DMA,
             pltpu.SemaphoreType.DMA((4,)),
             pltpu.SemaphoreType.DMA((4,)),
         ],
@@ -356,6 +364,14 @@
             flops=2_100_000_000, bytes_accessed=8_000_000, transcendentals=2000
         ),
     )(*operands)
+    fine_result, edge_result, coarse_result = pl.pallas_call(
+        hand_over,
+        out_shape=results,
+        in_specs=[in_vmem] * 3,
+        out_specs=(pl.BlockSpec(memory_space=pltpu.HBM),) * 3,
+        scratch_shapes=[pltpu.SemaphoreType.DMA((3,))],
+        compiler_params=pltpu.CompilerParams(vmem_limit_bytes=56 * 1024 * 1024),
+    )(*[pltpu.with_memory_space_constraint(h, pltpu.VMEM) for h in held])
     edge_result = edge_result.reshape(SLOTS, ROWS, WIDTH).transpose(1, 0, 2)
     return fine_result, edge_result, coarse_result
 

time: 62 us -> 57 us (0.919)
  local copies, waits for them, and re-layouts: 4.53 us -> 0 us
    unnamed x3 -> x0, local copies, waits for them, and re-layouts: 4.53 us -> none
    pallas_call x1 -> x2, Pallas kernels: 56.2 us -> 56.2 us  [the longest x1 55.4 us: shards(): pl.pallas_call(kernel, out_shape=tuple((pltpu.VMEM(r.shape, BF16) for r i...]
where the time goes in v2:
time: 57 us; the launch traced here: 56.8 us
  Pallas kernels  56.2 us (99%)
  between operations  0.65 us (1%)
    pallas_call x1, Pallas kernels, shards(): pl.pallas_call(kernel, out_shape=tuple((pltpu.VMEM(r.shape, BF16) for r i...  55.4 us

profile of v2, /device:TPU:1, one launch (start us, length us, event | category | flops | bytes accessed | tf_op | source)
XLA Modules:
  0.0 56.8 jit_solution(9623556927532624909)
XLA Ops:
  0.6 55.4 %shard_map.175 = (bf16[128,256]{1,0:T(8,128)(2,1)S(1)}, bf16[768,256]{1,0:T(8,128)(2,1)S(1)}, bf16[16,256]{1,0:T(8,128)(2,1)S(1)}) custom-call(bf16[128,256]{1,0:T(8,128)(2,1)} %nodes_hbm.1, bf16[768,256]{1,0:T(8,128)(2,1)} %bitcast.12, s32[6,128]{1,0:T(8,128)} %bitcast.15, s32[1,16,8,16]{3,2,1,0:T(8,128)} %bitcast.14, s32[1,2,64]{2,1,0:T(2,128)} %bitcast.19, ...), custom_call_target="tpu_custom_call" | custom-call | flops 2100000000 | bytes 8000000 | tf_op jit(solution)/shard_map/pallas_call | solution.py:335
  56.0 0.8 %shard_map.176 = (bf16[128,256]{1,0:T(8,128)(2,1)}, bf16[768,256]{1,0:T(8,128)(2,1)}, bf16[16,256]{1,0:T(8,128)(2,1)}) custom-call(bf16[128,256]{1,0:T(8,128)(2,1)S(1)} %get-tuple-element.9.refs_0_, bf16[768,256]{1,0:T(8,128)(2,1)S(1)} %get-tuple-element.10.refs_1_, bf16[16,256]{1,0:T(8,128)(2,1)S(1)} %get-tuple-element.11.refs_2_), custom_call_target="tpu_custom_call" | custom-call | tf_op jit(solution)/shard_map/pallas_call | solution.py:367

commit v3 on v2

--- a/solution.py
+++ b/solution.py
@@ -103,10 +103,11 @@
 
     def group_first(visit):
         def step(t, carry):
-            visit(lax.rem(hidden_at + t, HIDDEN))
+            away = (t + 1) >> 1
+            visit(lax.rem(hidden_at + HIDDEN // 2 + away * (1 - 2 * (t & 1)), HIDDEN))
             return carry
 
-        lax.fori_loop(1, HIDDEN, step, 0)
+        lax.fori_loop(0, HIDDEN - 1, step, 0)
 
     far_first(
         lambda p: pl.semaphore_signal(barrier, inc=1, device_id={"nodes": p}, device_id_type=MESH)
@@ -140,7 +141,20 @@
 
     pl.semaphore_wait(barrier, NODES - 1 + HIDDEN - 1)
 
-    def send(src, dst, which):
+    def low_first(visit):
+        def step(z, carry):
+            for dx in (2, 1, 3):
+                visit(lax.rem(x_at + dx, NX) * NZ + z)
+
+            @pl.when(z != z_at)
+            def _():
+                visit(x_at * NZ + z)
+
+            return carry
+
+        lax.fori_loop(0, NZ, step, 0)
+
+    def send(src, dst, which, order=far_first):
         def visit(p):
             pltpu.make_async_remote_copy(
                 src_ref=src.at[p],
@@ -151,7 +165,7 @@
                 device_id_type=MESH,
             ).start()
 
-        far_first(visit)
+        order(visit)
 
     def send_group(p):
         pltpu.make_async_remote_copy(
@@ -166,8 +180,8 @@
     def wait_all(buffer, count, sem):
         pltpu.make_async_copy(buffer.at[pl.ds(0, count)], buffer.at[pl.ds(0, count)], sem).wait()
 
+    group_first(send_group)
     send(ghost_src, ghost_dst, 1)
-    group_first(send_group)
 
     for i in range(3, 7):
         loads[i].wait()
@@ -287,7 +301,7 @@
     coarse_out[...] = coarse
 
     back_src[...] = dot(member_back, halves(coarse)).reshape(NODES, 8, 128).astype(BF16)
-    send(back_src, back_dst, 3)
+    send(back_src, back_dst, 3, low_first)
     back_dst[pl.ds(node_at, 1)] = back_src[pl.ds(node_at, 1)]
     wait_all(back_dst, NODES - 1, recv_sems.at[3])
 

time: 57 us -> 55.8 us (0.979)
  Pallas kernels: 56.2 us -> 55 us
    pallas_call x1, Pallas kernels: 55.4 us -> 54.2 us  [shards(): pl.pallas_call(kernel, out_shape=tuple((pltpu.VMEM(r.shape, BF16) for r i...]
where the time goes in v3:
time: 55.8 us; the launch traced here: 55.6 us
  Pallas kernels  55 us (99%)
  between operations  0.65 us (1%)
    pallas_call x1, Pallas kernels, shards(): pl.pallas_call(kernel, out_shape=tuple((pltpu.VMEM(r.shape, BF16) for r i...  54.2 us

profile of v3, /device:TPU:1, one launch (start us, length us, event | category | flops | bytes accessed | tf_op | source)
XLA Modules:
  0.0 55.6 jit_solution(10279645337643169108)
XLA Ops:
  0.6 54.2 %shard_map.175 = (bf16[128,256]{1,0:T(8,128)(2,1)S(1)}, bf16[768,256]{1,0:T(8,128)(2,1)S(1)}, bf16[16,256]{1,0:T(8,128)(2,1)S(1)}) custom-call(bf16[128,256]{1,0:T(8,128)(2,1)} %nodes_hbm.1, bf16[768,256]{1,0:T(8,128)(2,1)} %bitcast.12, s32[6,128]{1,0:T(8,128)} %bitcast.15, s32[1,16,8,16]{3,2,1,0:T(8,128)} %bitcast.14, s32[1,2,64]{2,1,0:T(2,128)} %bitcast.19, ...), custom_call_target="tpu_custom_call" | custom-call | flops 2100000000 | bytes 8000000 | tf_op jit(solution)/shard_map/pallas_call | solution.py:349
  54.8 0.8 %shard_map.176 = (bf16[128,256]{1,0:T(8,128)(2,1)}, bf16[768,256]{1,0:T(8,128)(2,1)}, bf16[16,256]{1,0:T(8,128)(2,1)}) custom-call(bf16[128,256]{1,0:T(8,128)(2,1)S(1)} %get-tuple-element.9.refs_0_, bf16[768,256]{1,0:T(8,128)(2,1)S(1)} %get-tuple-element.10.refs_1_, bf16[16,256]{1,0:T(8,128)(2,1)S(1)} %get-tuple-element.11.refs_2_), custom_call_target="tpu_custom_call" | custom-call | tf_op jit(solution)/shard_map/pallas_call | solution.py:381

commit v4 on v3

--- a/solution.py
+++ b/solution.py
@@ -97,7 +97,7 @@
                 visit(lax.rem(x_at + dx, NX) * NZ + lax.rem(z_at + dz, NZ))
             return carry
 
-        lax.fori_loop(0, NZ - 1, step, 0)
+        lax.fori_loop(0, NZ - 1, step, 0, unroll=5)
         for dx in (2, 1, 3):
             visit(lax.rem(x_at + dx, NX) * NZ + z_at)
 
@@ -107,7 +107,7 @@
             visit(lax.rem(hidden_at + HIDDEN // 2 + away * (1 - 2 * (t & 1)), HIDDEN))
             return carry
 
-        lax.fori_loop(0, HIDDEN - 1, step, 0)
+        lax.fori_loop(0, HIDDEN - 1, step, 0, unroll=5)
 
     far_first(
         lambda p: pl.semaphore_signal(barrier, inc=1, device_id={"nodes": p}, device_id_type=MESH)
@@ -152,7 +152,7 @@
 
             return carry
 
-        lax.fori_loop(0, NZ, step, 0)
+        lax.fori_loop(0, NZ, step, 0, unroll=4)
 
     def send(src, dst, which, order=far_first):
         def visit(p):
@@ -245,23 +245,23 @@
     node_part = dot(own, w_ni[:WIDTH, :])
     from_own = dot(take_own, own)
 
+    ghost_dst[pl.ds(node_at, 1)] = ghost_src[pl.ds(node_at, 1)]
+    wait_all(ghost_dst, NODES - 1, recv_sems.at[1])
+
+    def flat(buffer):
+        return buffer[...].astype(F32).reshape(MSG, 128).astype(BF16)
+
+    arrived = ghost_dst[...].astype(F32)
+    arrived = jnp.concatenate([arrived, jnp.zeros_like(arrived)], axis=1)
+    arrived = arrived.reshape(MSG, 128).astype(BF16)
+    ghosts = jnp.concatenate([dot(split, arrived) for split in ghost_split], axis=1).astype(BF16)
+    from_far = from_own + dot(take_ghost, ghosts)
     group_dst[pl.ds(hidden_at, 1)] = group_src[pl.ds(hidden_at, 1)]
     wait_all(group_dst, HIDDEN - 1, recv_sems.at[0])
     arrived = group_dst[...].reshape(HIDDEN * 16, 128)
     in_group = jnp.concatenate([dot(split, arrived) for split in group_split], axis=1).astype(BF16)
-    from_near = from_own + dot(take_group, in_group)
-
-    ghost_dst[pl.ds(node_at, 1)] = ghost_src[pl.ds(node_at, 1)]
-    wait_all(ghost_dst, NODES - 1, recv_sems.at[1])
-
-    def flat(buffer):
-        return buffer[...].astype(F32).reshape(MSG, 128).astype(BF16)
-
-    arrived = ghost_dst[...].astype(F32)
-    arrived = jnp.concatenate([arrived, jnp.zeros_like(arrived)], axis=1)
-    arrived = arrived.reshape(MSG, 128).astype(BF16)
-    ghosts = jnp.concatenate([dot(split, arrived) for split in ghost_split], axis=1).astype(BF16)
-    source = (from_near + dot(take_ghost, ghosts)).astype(BF16)
+    source = (from_far + dot(take_group, in_group)).astype(BF16)
+
     total = None
     for c in range(0, UNITS, WIDTH):
         hidden = first_part[:, c : c + WIDTH] + dot(source, w_ei[WIDTH : 2 * WIDTH, c : c + WIDTH])
@@ -316,7 +316,12 @@
 
 def hand_over(*refs):
     sems = refs[-1]
-    copies = [pltpu.make_async_copy(refs[i], refs[3 + i], sems.at[i]) for i in range(3)]
+    copies = [pltpu.make_async_copy(refs[i], refs[3 + i], sems.at[i]) for i in (0, 2)]
+    for k in range(SLOTS):
+        rows = pl.ds(k * ROWS, ROWS)
+        copies.append(
+            pltpu.make_async_copy(refs[1].at[rows], refs[4].at[rows], sems.at[3 + k])
+        )
     for copy in copies:
         copy.start()
     for copy in copies:
@@ -383,7 +388,7 @@
         out_shape=results,
         in_specs=[in_vmem] * 3,
         out_specs=(pl.BlockSpec(memory_space=pltpu.HBM),) * 3,
-        scratch_shapes=[pltpu.SemaphoreType.DMA((3,))],
+        scratch_shapes=[pltpu.SemaphoreType.DMA((3 + SLOTS,))],
         compiler_params=pltpu.CompilerParams(vmem_limit_bytes=56 * 1024 * 1024),
     )(*[pltpu.with_memory_space_constraint(h, pltpu.VMEM) for h in held])
     edge_result = edge_result.reshape(SLOTS, ROWS, WIDTH).transpose(1, 0, 2)

time: 55.8 us -> 55.3 us (level); the launches traced: 55.6 us -> 54.4 us
  Pallas kernels: 55 us -> 53.7 us
    pallas_call x1, Pallas kernels: 54.2 us -> 52.9 us  [shards(): pl.pallas_call(kernel, out_shape=tuple((pltpu.VMEM(r.shape, BF16) for r i...]
where the time goes in v4:
time: 55.3 us; the launch traced here: 54.4 us
  Pallas kernels  53.7 us (97%)
  between operations  0.65 us (1%)
    pallas_call x1, Pallas kernels, shards(): pl.pallas_call(kernel, out_shape=tuple((pltpu.VMEM(r.shape, BF16) for r i...  52.9 us

profile of v4, /device:TPU:1, one launch (start us, length us, event | category | flops | bytes accessed | tf_op | source)
XLA Modules:
  0.0 54.4 jit_solution(13340708756458054075)
XLA Ops:
  0.6 52.9 %shard_map.175 = (bf16[128,256]{1,0:T(8,128)(2,1)S(1)}, bf16[768,256]{1,0:T(8,128)(2,1)S(1)}, bf16[16,256]{1,0:T(8,128)(2,1)S(1)}) custom-call(bf16[128,256]{1,0:T(8,128)(2,1)} %nodes_hbm.1, bf16[768,256]{1,0:T(8,128)(2,1)} %bitcast.12, s32[6,128]{1,0:T(8,128)} %bitcast.15, s32[1,16,8,16]{3,2,1,0:T(8,128)} %bitcast.14, s32[1,2,64]{2,1,0:T(2,128)} %bitcast.19, ...), custom_call_target="tpu_custom_call" | custom-call | flops 2100000000 | bytes 8000000 | tf_op jit(solution)/shard_map/pallas_call | solution.py:354
  53.5 0.8 %shard_map.176 = (bf16[128,256]{1,0:T(8,128)(2,1)}, bf16[768,256]{1,0:T(8,128)(2,1)}, bf16[16,256]{1,0:T(8,128)(2,1)}) custom-call(bf16[128,256]{1,0:T(8,128)(2,1)S(1)} %get-tuple-element.9.refs_0_, bf16[768,256]{1,0:T(8,128)(2,1)S(1)} %get-tuple-element.10.refs_1_, bf16[16,256]{1,0:T(8,128)(2,1)S(1)} %get-tuple-element.11.refs_2_), custom_call_target="tpu_custom_call" | custom-call | tf_op jit(solution)/shard_map/pallas_call | solution.py:386
